TPU v7x, 256 devices: a whole 4x4x8 slice. The times are simulated.
256 devices in a mesh: batch: 8 (over y, z_lo), seq: 32 (over z_hi, x, core).
Axes of the slice: x: 4, y: 4, z: 8 (z_hi: 4, z_lo: 2; z = z_hi * 2 + z_lo), core: 2. Of those that a mesh axis runs over, the one named last changes fastest.
Arguments:
- tokens: bfloat16 [2048, 256, 768], P(('batch', 'seq')), parts along dimension 0, may hold values from -6 to 6
- cotangent: bfloat16 [2048, 256, 768], P(('batch', 'seq')), parts along dimension 0, may hold values from -6 to 6
- gate_taps: float32 [3, 768], replicated, may hold values from -3.5 to 3.5
- key_taps: float32 [3, 768], replicated, may hold values from -3.5 to 3.5
- value_taps: float32 [3, 768], replicated, may hold values from -3.5 to 3.5
- inner_mix: bfloat16 [256, 256], replicated, may hold values from -0.375 to 0.375
- outer_mix: bfloat16 [256, 256], replicated, may hold values from -0.375 to 0.375
- spectrum: float32 [256, 768], replicated, may hold values from 0.5 to 2
Outputs:
- grad_tokens: bfloat16 [2048, 256, 768], P(('batch', 'seq')), parts along dimension 0
- grad_gate_taps: float32 [24, 768], P('batch'), parts along dimension 0
- grad_key_taps: float32 [24, 768], P('batch'), parts along dimension 0
- grad_value_taps: float32 [24, 768], P('batch'), parts along dimension 0
- grad_inner_mix: float32 [2048, 256], P('batch'), parts along dimension 0
- grad_outer_mix: float32 [2048, 256], P('batch'), parts along dimension 0
- grad_spectrum: float32 [2048, 768], P('batch'), parts along dimension 0
There are 8 independent parts, one for each index of `batch`. A program takes and returns all parts, laid end to end along the dimension named above; an argument that names none is the same for every part. Nothing has to cross between parts.
All inputs are finite; a program needn't handle non-finite values.
Results may differ from a plain program's by a relative error of at most 0.0064.
Values may be sent and summed in bfloat16 or wider, within the bound.
A program may use at most 128 MiB of HBM per device.

v0:
```python
import jax
import jax.numpy as jnp
from jax import lax
from jax.sharding import PartitionSpec as P


def shifted(value, axis, steps):
    count = lax.axis_size(axis)
    first, last = (max(0, -steps), min(count, count - steps))
    return lax.ppermute(value, axis, [(source, source + steps) for source in range(first, last)])


def causal_matrix(weights):
    extent = weights.shape[0]
    lower_part = jnp.tril(jnp.ones((extent, extent), jnp.bool_), -1)
    return jnp.where(lower_part, weights, jnp.eye(extent, dtype=weights.dtype))


def strict_lower(extent):
    return jnp.tril(jnp.ones((extent, extent), jnp.float32), -1)


def conv_forward(padded, taps):
    return (
        taps[0] * padded[2:].astype(jnp.float32)
        + taps[1] * padded[1:-1].astype(jnp.float32)
        + taps[2] * padded[:-2].astype(jnp.float32)
    )


def conv_backward(padded_grad, taps):
    return taps[0] * padded_grad[:-2] + taps[1] * padded_grad[1:-1] + taps[2] * padded_grad[2:]


def taps_grad(grad_rows, padded):
    count = grad_rows.shape[0]
    return jnp.stack(
        [
            jnp.sum(
                grad_rows * padded[2 - shift_by : 2 - shift_by + count].astype(jnp.float32), axis=0
            )
            for shift_by in range(3)
        ]
    )


def body(tokens, cotangent, gate_taps, key_taps, value_taps, inner_mix, outer_mix, spectrum):
    block_count, block_len, channels = tokens.shape
    token_rows = tokens.reshape(block_count * block_len, channels)
    before = shifted(token_rows[-2:], "seq", 1)
    padded = jnp.concatenate([before, token_rows], 0)
    gate_conv = conv_forward(padded, gate_taps)
    key_conv = conv_forward(padded, key_taps)
    value_conv = conv_forward(padded, value_taps)
    product = (key_conv * value_conv).astype(jnp.bfloat16).reshape(block_count, block_len, channels)
    first_mix = causal_matrix(inner_mix)
    second_mix = causal_matrix(outer_mix)
    pre_scale = jnp.einsum("jk,ikc->ijc", first_mix, product, preferred_element_type=jnp.float32)
    inner_out = (pre_scale * spectrum).astype(jnp.bfloat16)
    grad_mixed = (cotangent * gate_conv.reshape(block_count, block_len, channels)).astype(
        jnp.bfloat16
    )
    column_piece = lax.all_to_all(inner_out, "seq", split_axis=1, concat_axis=0, tiled=True)
    mixed_piece = jnp.einsum(
        "ik,kjc->ijc", second_mix, column_piece, preferred_element_type=jnp.float32
    )
    mixed_cols = mixed_piece.astype(jnp.bfloat16)
    mixed_out = lax.all_to_all(mixed_cols, "seq", split_axis=0, concat_axis=1, tiled=True)
    grad_cols = lax.all_to_all(grad_mixed, "seq", split_axis=1, concat_axis=0, tiled=True)
    grad_inner_cols = jnp.einsum(
        "ki,kjc->ijc", second_mix, grad_cols, preferred_element_type=jnp.float32
    ).astype(jnp.bfloat16)
    grad_inner = lax.all_to_all(grad_inner_cols, "seq", split_axis=0, concat_axis=1, tiled=True)
    outer_term = jnp.einsum(
        "ijc,kjc->ik", grad_cols, column_piece, preferred_element_type=jnp.float32
    ) * strict_lower(second_mix.shape[0])
    spectrum_term = jnp.sum(grad_inner.astype(jnp.float32) * pre_scale, axis=0)
    grad_scaled = (grad_inner * spectrum).astype(jnp.bfloat16)
    inner_term = jnp.einsum(
        "ijc,ikc->jk", grad_scaled, product, preferred_element_type=jnp.float32
    ) * strict_lower(block_len)
    grad_product = jnp.einsum(
        "jk,ijc->ikc", first_mix, grad_scaled, preferred_element_type=jnp.float32
    ).reshape(block_count * block_len, channels)
    grad_gate = (cotangent * mixed_out.astype(jnp.float32)).reshape(
        block_count * block_len, channels
    )
    grad_key = grad_product * value_conv
    grad_value = grad_product * key_conv
    after_gate, after_key, after_value = shifted(
        (grad_gate[:2], grad_key[:2], grad_value[:2]), "seq", -1
    )
    grad_rows = conv_backward(jnp.concatenate([grad_gate, after_gate], 0), gate_taps)
    grad_rows = grad_rows + conv_backward(jnp.concatenate([grad_key, after_key], 0), key_taps)
    grad_rows = grad_rows + conv_backward(jnp.concatenate([grad_value, after_value], 0), value_taps)
    grad_tokens = grad_rows.reshape(block_count, block_len, channels).astype(jnp.bfloat16)
    totals = lax.psum(
        (
            taps_grad(grad_gate, padded),
            taps_grad(grad_key, padded),
            taps_grad(grad_value, padded),
            inner_term,
            outer_term,
            spectrum_term,
        ),
        "seq",
    )
    return (grad_tokens, totals[0], totals[1], totals[2], totals[3], totals[4], totals[5])


def solution(mesh):
    in_specs = (
        P(("batch", "seq"), None, None),
        P(("batch", "seq"), None, None),
        P(),
        P(),
        P(),
        P(),
        P(),
        P(),
    )
    out_specs = (
        P(("batch", "seq"), None, None),
        P("batch", None),
        P("batch", None),
        P("batch", None),
        P("batch", None),
        P("batch", None),
        P("batch", None),
    )
    return jax.shard_map(body, mesh=mesh, in_specs=in_specs, out_specs=out_specs, check_vma=False)
```

profile of v0, /device:TPU:8, one launch (start us, length us, event | category | flops | bytes accessed | tf_op | source)
XLA Modules:
  0.0 844.6 jit_solution(12262168385228112533)
XLA Ops:
  7.2 0.0 copy-start
  7.2 0.9 slice.103
  8.0 1.9 collective-permute-start
  9.9 0.9 slice_reduce_fusion.4
  10.8 0.8 slice_reduce_fusion.8
  11.7 0.0 collective-permute-done
  11.7 8.0 multiply_convert_fusion.1
  19.6 2.1 fusion.21
  21.7 0.9 copy-done.6
  22.7 0.7 fusion.15
  23.4 0.0 copy-start.10
  23.4 3.4 copy.63
  26.8 14.6 %all-to-all-start.2 = ((bf16[8,256,768]{2,0,1:T(8,128)(2,1)}), bf16[8,256,768]{2,0,1:T(8,128)(2,1)}, u32[]{:S(2)}, u32[]{:S(2)}) async-start(bf16[8,256,768]{2,0,1:T(8,128)(2,1)} %copy.63), calls=%async_computation.2 | async-start | bytes 6291456 | tf_op jit(solution)/shard_map/all_to_all | solution.py:69
  41.4 69.7 %all-to-all-done.2 = bf16[8,256,768]{2,0,1:T(8,128)(2,1)} async-done(((bf16[8,256,768]{2,0,1:T(8,128)(2,1)}), bf16[8,256,768]{2,0,1:T(8,128)(2,1)}, u32[]{:S(2)}, u32[]{:S(2)}) %all-to-all-start.2) | async-done | bytes 3145760 | tf_op jit(solution)/shard_map/all_to_all | solution.py:69
  111.2 3.0 fusion.50
  114.1 3.4 copy.66
  117.5 9.2 %all-to-all-start.3 = ((bf16[256,8,768]{2,1,0:T(8,128)(2,1)}), bf16[256,8,768]{2,1,0:T(8,128)(2,1)}, u32[]{:S(2)}, u32[]{:S(2)}) async-start(bf16[256,8,768]{2,1,0:T(8,128)(2,1)} %copy.66), calls=%async_computation.3 | async-start | bytes 6291456 | tf_op jit(solution)/shard_map/all_to_all | solution.py:73
  126.7 2.3 copy.57
  129.0 72.1 %all-to-all-done.3 = bf16[256,8,768]{2,1,0:T(8,128)(2,1)} async-done(((bf16[256,8,768]{2,1,0:T(8,128)(2,1)}), bf16[256,8,768]{2,1,0:T(8,128)(2,1)}, u32[]{:S(2)}, u32[]{:S(2)}) %all-to-all-start.3) | async-done | bytes 3145760 | tf_op jit(solution)/shard_map/all_to_all | solution.py:73
  201.1 5.1 copy_bitcast_fusion
  206.2 6.6 copy.68
  212.7 7.9 fusion.34
  220.6 5.1 copy.58
  225.7 63.3 %all_to_all.54 = bf16[8,256,768]{2,0,1:T(8,128)(2,1)S(1)} all-to-all(bf16[8,256,768]{2,0,1:T(8,128)(2,1)} %copy.58), channel_id=1, replica_groups=mesh['batch'=8,'seq'=32] {'seq'}, dimensions={1} | all-to-all | bytes 6291456 | tf_op jit(solution)/shard_map/all_to_all | solution.py:63
  289.0 1.7 copy-done.7
  290.7 1.0 fusion.47
  291.7 3.4 copy.61
  295.1 20.2 %all-to-all-start.1 = ((bf16[256,8,768]{2,1,0:T(8,128)(2,1)}), bf16[256,8,768]{2,1,0:T(8,128)(2,1)}, u32[]{:S(2)}, u32[]{:S(2)}) async-start(bf16[256,8,768]{2,1,0:T(8,128)(2,1)} %copy.61), calls=%async_computation.1 | async-start | bytes 6291456 | tf_op jit(solution)/shard_map/all_to_all | solution.py:68
  315.3 0.3 all-reduce.4.cloned.1.call-start
  315.5 5.8 fusion.58
  321.3 3.9 fusion.59
  325.3 0.0 all-reduce.4.cloned.1.call-update
  325.3 6.8 fusion.64
  332.1 314.6 %all-reduce.4.cloned.1.call-done = (f32[256,256]{1,0:T(8,128)}, f32[256,256]{1,0:T(8,128)}, f32[256,768]{0,1:T(8,128)}) async-done(((f32[256,256]{1,0:T(8,128)}, f32[256,256]{1,0:T(8,128)}, f32[256,768]{0,1:T(8,128)}), (f32[256,256]{1,0:T(8,128)}, f32[256,256]{1,0:T(8,128)}, f32[256,768]{0,1:T(8,128)})) %all-reduce.4.cloned.1.call-update) | async-done | bytes 1310736 | tf_op jit(solution)/shard_map/psum | solution.py:97
  646.7 2.3 copy.73
  649.0 0.0 all-to-all-done.1
  649.0 2.7 bitcast_convert_fusion
  651.7 3.5 multiply_reduce_fusion
  655.2 10.1 %fusion.22 = (f32[768]{0:T(1024)S(1)}, f32[768]{0:T(1024)S(1)}, f32[768]{0:T(1024)S(1)}, f32[768]{0:T(1024)S(1)}, f32[768]{0:T(1024)S(1)}, /*index=5*/f32[768]{0...) fusion(bf16[8,256,768]{2,1,0:T(8,128)(2,1)S(1)} %copy-done, ...), kind=kLoop, calls=%fused_computation.47 | loop fusion | flops 55044096 | bytes 34649088 | tf_op jit(solution)/shard_map/reduce_sum | solution.py:39
  665.5 1.3 collective-permute-start.2
  666.8 1.3 collective-permute-start.3
  668.1 1.3 collective-permute-start.1
  669.4 0.4 copy-done.5
  669.9 144.2 %all-reduce = (f32[3,768]{1,0:T(4,128)}, f32[3,768]{1,0:T(4,128)}, f32[3,768]{1,0:T(4,128)}) all-reduce(f32[3,768]{1,0:T(4,128)S(1)} %pad_maximum_fusion.4, f32[3,768]{1,0:T(4,128)S(1)} %pad_maximum_fusion.5, f32[3,768]{1,0:T(4,128)S(1)} %pad_maximum_fusion.6), channel_id=1, replica_groups=mesh['batch'=8,'seq'=32] {'seq'}, use_global_device_ids=true, to_apply=%region_3.4 | all-reduce | flops 6912 | bytes 55296 | tf_op jit(solution)/shard_map/psum | solution.py:97
  814.1 0.0 collective-permute-done.2
  814.2 22.1 %fusion.5 = bf16[2048,768]{1,0:T(8,128)(2,1)} fusion(f32[2048,768]{1,0:T(8,128)} %copy-done.5, f32[2,768]{1,0:T(2,128)S(1)} %collective-permute-done.3, f32[2048,768]{1,0:T(8,128)} %copy-done.4, f32[2,768]{1,0:T(2,128)S(1)} %collective-permute-done.2, f32[2048,768]{1,0:T(8,128)} %bitcast.93, f32[2,768]{1,0:T(2,128)S(1)} %collective-permute-done.1, ...), kind=kLoop, calls=%fused_computation.30 | loop fusion | flops 37748736 | bytes 22066176 | tf_op jit(solution)/shard_map/convert_element_type | solution.py:96
  836.3 0.7 copy.116
  837.0 0.7 copy.117
  (39 shorter events, 0.1 us)
Async XLA Ops:
  7.2 12.5 %copy-start = (bf16[8,256,768]{2,1,0:T(8,128)(2,1)S(1)}, bf16[8,256,768]{2,1,0:T(8,128)(2,1)}, u32[]{:S(2)}) copy-start(bf16[8,256,768]{2,1,0:T(8,128)(2,1)} %param.8) | copy-start | bytes 9437188
  8.0 3.6 collective-permute-start
  19.6 2.1 copy-start.2
  19.6 3.0 copy-start.6
  23.4 87.8 %copy-start.10 = (bf16[256,256]{1,0:T(8,128)(2,1)S(1)}, bf16[256,256]{1,0:T(8,128)(2,1)}, u32[]{:S(2)}) copy-start(bf16[256,256]{1,0:T(8,128)(2,1)} %param.14) | copy-start | bytes 393220
  26.8 84.3 %all-to-all-start.2 = ((bf16[8,256,768]{2,0,1:T(8,128)(2,1)}), bf16[8,256,768]{2,0,1:T(8,128)(2,1)}, u32[]{:S(2)}, u32[]{:S(2)}) async-start(bf16[8,256,768]{2,0,1:T(8,128)(2,1)} %copy.63), calls=%async_computation.2 | async-start | bytes 6291456 | tf_op jit(solution)/shard_map/all_to_all | solution.py:69
  117.5 83.6 %all-to-all-start.3 = ((bf16[256,8,768]{2,1,0:T(8,128)(2,1)}), bf16[256,8,768]{2,1,0:T(8,128)(2,1)}, u32[]{:S(2)}, u32[]{:S(2)}) async-start(bf16[256,8,768]{2,1,0:T(8,128)(2,1)} %copy.66), calls=%async_computation.3 | async-start | bytes 6291456 | tf_op jit(solution)/shard_map/all_to_all | solution.py:73
  206.2 6.6 copy-start.9
  289.0 1.7 copy-start.7
  295.1 353.9 %all-to-all-start.1 = ((bf16[256,8,768]{2,1,0:T(8,128)(2,1)}), bf16[256,8,768]{2,1,0:T(8,128)(2,1)}, u32[]{:S(2)}, u32[]{:S(2)}) async-start(bf16[256,8,768]{2,1,0:T(8,128)(2,1)} %copy.61), calls=%async_computation.1 | async-start | bytes 6291456 | tf_op jit(solution)/shard_map/all_to_all | solution.py:68
  315.3 331.5 %all-reduce.4.cloned.1.call-start = ((), (), s32[]{:S(2)}) async-start(), calls=%async_computation.4 | async-start | bytes 2621440 | tf_op jit(solution)/shard_map/psum | solution.py:97
  315.5 5.8 copy-start.8
  651.7 3.6 copy-start.3
  655.2 12.9 %copy-start.1 = (f32[8,256,768]{2,1,0:T(8,128)}, f32[8,256,768]{2,1,0:T(8,128)S(1)}, u32[]{:S(2)}) copy-start(f32[8,256,768]{2,1,0:T(8,128)S(1)} %get-tuple-element.50) | copy-start | bytes 18874372
  665.3 2.8 copy-start.4
  665.3 4.5 copy-start.5
  665.5 148.7 %collective-permute-start.2 = (f32[2,768]{1,0:T(2,128)S(1)}, f32[2,768]{1,0:T(2,128)S(1)}, u32[]{:S(2)}, u32[]{:S(2)}) collective-permute-start(f32[2,768]{1,0:T(2,128)S(1)} %slice.109), channel_id=1, source_target_pairs={{1,0},{2,1},{3,2},{4,3},{5,4},{6,5},{7,6},{8,7},{9,8},{10,9},{11,1... | collective-permute-start | bytes 18440 | tf_op jit(solution)/shard_map/ppermute | solution.py:10
  666.8 147.4 %collective-permute-start.3 = (f32[2,768]{1,0:T(2,128)S(1)}, f32[2,768]{1,0:T(2,128)S(1)}, u32[]{:S(2)}, u32[]{:S(2)}) collective-permute-start(f32[2,768]{1,0:T(2,128)S(1)} %slice.112), channel_id=1, source_target_pairs={{1,0},{2,1},{3,2},{4,3},{5,4},{6,5},{7,6},{8,7},{9,8},{10,9},{11,1... | collective-permute-start | bytes 18440 | tf_op jit(solution)/shard_map/ppermute | solution.py:10
  668.1 146.1 %collective-permute-start.1 = (f32[2,768]{1,0:T(2,128)S(1)}, f32[2,768]{1,0:T(2,128)S(1)}, u32[]{:S(2)}, u32[]{:S(2)}) collective-permute-start(f32[2,768]{1,0:T(2,128)S(1)} %slice.106), channel_id=1, source_target_pairs={{1,0},{2,1},{3,2},{4,3},{5,4},{6,5},{7,6},{8,7},{9,8},{10,9},{11,1... | collective-permute-start | bytes 18440 | tf_op jit(solution)/shard_map/ppermute | solution.py:10
  814.1 22.2 %copy-start.12 = (f32[256,256]{1,0:T(8,128)S(1)}, f32[256,256]{1,0:T(8,128)}, u32[]{:S(2)}) copy-start(f32[256,256]{1,0:T(8,128)} %get-tuple-element.64) | copy-start | bytes 786436
  814.1 22.9 %copy-start.11 = (f32[256,256]{1,0:T(8,128)S(1)}, f32[256,256]{1,0:T(8,128)}, u32[]{:S(2)}) copy-start(f32[256,256]{1,0:T(8,128)} %get-tuple-element.65) | copy-start | bytes 786436
Sparse Core Ops, SparseCore 0:
  325.4 321.2 all-reduce.3
where the time goes:
time: 846 us; the launch traced here: 845 us
  waiting for transfers between devices  457 us (54%)
  blocking collectives  208 us (25%)
  other arithmetic  54.3 us (6%)
  starting transfers between devices  49.9 us (6%)
  local copies, waits for them, and re-layouts  33.6 us (4%)
  matrix products  28.4 us (3%)
  between operations  14.4 us (2%)
    psum x1, waiting for transfers between devices, body(): lax.psum((taps_grad(grad_gate, padded), taps_grad(grad_key, padded), taps...  315 us
    psum x1, blocking collectives, body(): lax.psum((taps_grad(grad_gate, padded), taps_grad(grad_key, padded), taps...  144 us
    all_to_all x1, waiting for transfers between devices, body(): lax.all_to_all(grad_inner_cols, 'seq', split_axis=0, concat_axis=1, tiled...  72.1 us
    all_to_all x1, waiting for transfers between devices, body(): lax.all_to_all(grad_mixed, 'seq', split_axis=1, concat_axis=0, tiled=True)  69.7 us
    all_to_all x1, blocking collectives, body(): lax.all_to_all(inner_out, 'seq', split_axis=1, concat_axis=0, tiled=True)  63.3 us
    convert_element_type x1, other arithmetic, body(): grad_rows.reshape(block_count, block_len, channels).astype(jnp.bfloat16)  22.1 us
    all_to_all x1, starting transfers between devices, body(): lax.all_to_all(mixed_cols, 'seq', split_axis=0, concat_axis=1, tiled=True)  20.2 us
  transfers between devices with their start and end apart: 8, of which 3 were waited for; matrix products, arithmetic and copies ran while one was open for 3% of the time, Pallas kernels for 0%

commit v1 on v0

v1 whole, which is shorter than its diff:
```python
import jax
import jax.numpy as jnp
from jax import lax
from jax.experimental import pallas as pl
from jax.experimental.pallas import tpu as pltpu
from jax.sharding import PartitionSpec as P

MESH = pl.DeviceIdType.MESH
F32 = jnp.float32
BF16 = jnp.bfloat16

LEN = 256
CHIPS = 16
LANES = 128
CHUNKS = 3
HALF = LANES * CHUNKS
ROWS = CHIPS * LEN
OWN = ROWS // 2
HALO = 16


def dot(a, b):
    return jnp.dot(a, b, preferred_element_type=F32)


def dot_lanes(a, b):
    return lax.dot_general(a, b, (((1,), (1,)), ((), ())), preferred_element_type=F32)


def strict_lower(value, first_row):
    rows = lax.broadcasted_iota(jnp.int32, value.shape, 0) + first_row
    cols = lax.broadcasted_iota(jnp.int32, value.shape, 1)
    return jnp.where(rows > cols, value, 0.0)


def kernel(
    tok, cot, gate_taps, key_taps, value_taps, inner_mix, outer_mix, spectrum,
    out_tok, out_gate, out_key, out_value, out_inner, out_outer, out_spec,
    T, CT, PR, AB, S, Z, R, F, GT, MAT, CARRY, HB, HR, LB, TA,
    inner_acc, outer_acc, SG, sib_sum, red_send, red_recv, red_sum, gathered, gathered_sib,
    sg_all, sg_sib,
    in_sem, in_send, halo_sem, halo_send, z_sem, s_send, f_sem, r_send, hb_sem, hb_send,
    out_local, out_send, out_recv, sib_sem, sib_send, rs_sem, rs_send, ag_sem, ag_send,
    gx_sem, gx_send, sg_sem, sg_send, sgx_sem, sgx_send,
):
    batch = lax.axis_index("batch")
    seq = lax.axis_index("seq")
    core = seq % 2
    chip = seq // 2
    cz = chip // 4
    cx = chip % 4
    other = 1 - core
    sibling = (batch, chip * 2 + other)

    def chip_dev(q):
        return (batch, q * 2 + core)

    def peer(d):
        return ((cz + d // 4) % 4) * 4 + (cx + d % 4) % 4

    barrier = pltpu.get_barrier_semaphore()

    def greet(d, carry):
        pl.semaphore_signal(barrier, inc=1, device_id=chip_dev(peer(d)), device_id_type=MESH)
        return carry

    lax.fori_loop(1, CHIPS, greet, 0)
    pl.semaphore_signal(barrier, inc=1, device_id=sibling, device_id_type=MESH)
    pl.semaphore_wait(barrier, CHIPS)

    def remote(src, dst, send, recv, device):
        return pltpu.make_async_remote_copy(
            src_ref=src, dst_ref=dst, send_sem=send, recv_sem=recv,
            device_id=device, device_id_type=MESH,
        )

    def wait_bytes(ref, sem):
        pltpu.make_async_copy(ref, ref, sem).wait()

    my_rows = pl.ds(pl.multiple_of(core * OWN, OWN), OWN)
    halo_rows = pl.ds(pl.multiple_of(HALO + core * OWN, HALO), OWN)

    def lanes_of(c, ch):
        return pl.ds(pl.multiple_of(c * HALF + ch * LANES, LANES), LANES)

    def start_inputs(ch, carry):
        remote(tok.at[:, lanes_of(other, ch)], T.at[ch, halo_rows], in_send.at[ch, 0], in_sem.at[ch, 0], sibling).start()
        remote(cot.at[:, lanes_of(other, ch)], CT.at[ch, my_rows], in_send.at[ch, 1], in_sem.at[ch, 1], sibling).start()
        pltpu.make_async_copy(tok.at[:, lanes_of(core, ch)], T.at[ch, halo_rows], in_sem.at[ch, 0]).start()
        pltpu.make_async_copy(cot.at[:, lanes_of(core, ch)], CT.at[ch, my_rows], in_sem.at[ch, 1]).start()
        return carry

    lax.fori_loop(0, CHUNKS, start_inputs, 0)

    row_id = lax.broadcasted_iota(jnp.int32, (LEN, LEN), 0)
    col_id = lax.broadcasted_iota(jnp.int32, (LEN, LEN), 1)
    for at, weights in ((0, inner_mix), (2, outer_mix)):
        full = jnp.where(
            row_id > col_id, weights[...].astype(F32), jnp.where(row_id == col_id, 1.0, 0.0)
        )
        MAT[at] = full.astype(BF16)
        MAT[at + 1] = jnp.transpose(full).astype(BF16)
    MAT[4] = jnp.where(col_id == (row_id % 16) * 16 + row_id // 16, 1.0, 0.0).astype(BF16)
    inner_acc[...] = jnp.zeros_like(inner_acc)
    outer_acc[...] = jnp.zeros_like(outer_acc)
    TA[...] = jnp.zeros_like(TA)

    def send_halo(ch, carry):
        wait_bytes(T.at[ch, pl.ds(HALO, ROWS)], in_sem.at[ch, 0])

        @pl.when(chip < CHIPS - 1)
        def _():
            remote(
                T.at[ch, pl.ds(ROWS, HALO)], T.at[ch, pl.ds(0, HALO)],
                halo_send.at[ch], halo_sem.at[ch], chip_dev(chip + 1),
            ).start()

        @pl.when(chip == 0)
        def _():
            T[ch, 0:HALO] = jnp.zeros((HALO, LANES), BF16)

        wait_bytes(CT.at[ch], in_sem.at[ch, 1])
        return carry

    def taps_of(ref, ch):
        block = ref[:, lanes_of(core, ch)]
        return block[0:1], block[1:2], block[2:3]

    def shifted_rows(ch, i):
        ext = T[ch, pl.ds(pl.multiple_of(i * LEN, LEN), LEN + HALO)].astype(F32)
        return ext[HALO:], pltpu.roll(ext, 1, 0)[HALO:], pltpu.roll(ext, 2, 0)[HALO:]

    def conv(taps, x):
        return taps[0] * x[0] + taps[1] * x[1] + taps[2] * x[2]

    def block_rows(i):
        return pl.ds(pl.multiple_of(i * LEN, LEN), LEN)

    def before(ch, carry):
        gt, kt, vt = taps_of(gate_taps, ch), taps_of(key_taps, ch), taps_of(value_taps, ch)
        send_halo(ch, 0)

        def pair(step, c):
            p = CHIPS // 2 - 1 - step

            @pl.when(jnp.logical_and(p == 0, chip > 0))
            def _():
                wait_bytes(T.at[ch, pl.ds(0, HALO)], halo_sem.at[ch])

            products = []
            for b in range(2):
                i = 2 * p + b
                x = shifted_rows(ch, i)
                product = (conv(kt, x) * conv(vt, x)).astype(BF16)
                PR[ch, block_rows(i)] = product
                products.append(product)
                grad_mixed = CT[ch, block_rows(i)].astype(F32) * conv(gt, x)
                AB[i, :, LANES:] = grad_mixed.astype(BF16)
            pre = dot(MAT[0], jnp.concatenate(products, 1))
            scale = spectrum[:, lanes_of(core, ch)]
            for b in range(2):
                AB[2 * p + b, :, :LANES] = (pre[:, b * LANES:(b + 1) * LANES] * scale).astype(BF16)
            return c

        lax.fori_loop(0, CHIPS // 2, pair, 0)

        def regroup(j, c):
            rows = AB[:, pl.ds(pl.multiple_of(j * 16, 16), 16)].reshape(LEN, 2 * LANES)
            S[ch, j] = dot(MAT[4], rows).astype(BF16).reshape(16, 16, 2 * LANES)
            return c

        lax.fori_loop(0, CHIPS, regroup, 0)
        mine = pl.ds(pl.multiple_of(chip * 16, 16), 16)

        def send(d, c):
            q = peer(d)
            remote(S.at[ch, q], Z.at[ch, :, mine], s_send.at[ch], z_sem.at[ch], chip_dev(q)).start()
            return c

        lax.fori_loop(1, CHIPS, send, 0)
        pltpu.make_async_copy(S.at[ch, chip], Z.at[ch, :, mine], z_sem.at[ch]).start()
        return carry

    lax.fori_loop(0, CHUNKS, before, 0)

    def across(ch, carry):
        wait_bytes(Z.at[ch], z_sem.at[ch])
        scale = spectrum[pl.ds(pl.multiple_of(chip * 16, 16), 16), lanes_of(core, ch)]

        def pair(p, c):
            j = 2 * p
            z0, z1 = Z[ch, j], Z[ch, j + 1]
            inner = jnp.concatenate([z0[:, :LANES], z1[:, :LANES]], 1)
            grads = jnp.concatenate([z0[:, LANES:], z1[:, LANES:]], 1)
            mixed = dot(MAT[2], inner).astype(BF16)
            grad_inner = dot(MAT[3], grads).astype(BF16)
            outer_acc[...] += dot_lanes(grads, inner)
            terms = jnp.sum(grad_inner.astype(F32) * inner.astype(F32), axis=0, keepdims=True)
            for b in range(2):
                at = slice(b * LANES, (b + 1) * LANES)
                R[ch, j + b, :, :LANES] = mixed[:, at]
                R[ch, j + b, :, LANES:] = grad_inner[:, at]
                SG[ch, pl.ds(j + b, 1)] = terms[:, at]
            return c

        lax.fori_loop(0, 8, pair, 0)
        SG[ch] = SG[ch] / scale

        def send(d, c):
            q = peer(d)
            remote(
                R.at[ch, :, pl.ds(pl.multiple_of(q * 16, 16), 16)], F.at[ch, chip],
                r_send.at[ch], f_sem.at[ch], chip_dev(q),
            ).start()
            return c

        lax.fori_loop(1, CHIPS, send, 0)
        pltpu.make_async_copy(
            R.at[ch, :, pl.ds(pl.multiple_of(chip * 16, 16), 16)], F.at[ch, chip], f_sem.at[ch]
        ).start()
        return carry

    lax.fori_loop(0, CHUNKS, across, 0)

    half_rows = pl.ds(pl.multiple_of(core * 128, 128), 128)
    other_rows = pl.ds(pl.multiple_of(other * 128, 128), 128)

    def sibling_sum_start(k, acc):
        remote(acc.at[other_rows], sib_sum.at[k], sib_send.at[k], sib_sem.at[k], sibling).start()

    def scatter_start(k, acc, extra):
        wait_bytes(sib_sum.at[k], sib_sem.at[k])
        total = acc[half_rows] + sib_sum[k]
        red_send[k, :, 0:8] = total.reshape(CHIPS, 8, LEN)
        red_send[k, :, 8:16] = jnp.zeros((CHIPS, 8, LEN), F32)
        extra()

        def send(d, c):
            q = peer(d)
            remote(red_send.at[k, q], red_recv.at[k, chip], rs_send.at[k], rs_sem.at[k], chip_dev(q)).start()
            return c

        lax.fori_loop(1, CHIPS, send, 0)
        pltpu.make_async_copy(red_send.at[k, chip], red_recv.at[k, chip], rs_sem.at[k]).start()

    def gather_start(k):
        wait_bytes(red_recv.at[k], rs_sem.at[k])
        red_sum[k] = jnp.sum(red_recv[k], axis=0)

        def send(d, c):
            remote(red_sum.at[k], gathered.at[k, chip], ag_send.at[k], ag_sem.at[k], chip_dev(peer(d))).start()
            return c

        lax.fori_loop(1, CHIPS, send, 0)
        pltpu.make_async_copy(red_sum.at[k], gathered.at[k, chip], ag_sem.at[k]).start()

    def swap_start(k):
        wait_bytes(gathered.at[k], ag_sem.at[k])
        remote(gathered.at[k], gathered_sib.at[k], gx_send.at[k], gx_sem.at[k], sibling).start()

    def write_matrix(k, out):
        wait_bytes(gathered_sib.at[k], gx_sem.at[k])
        out[half_rows] = strict_lower(gathered[k, :, 0:8].reshape(128, LEN), core * 128)
        out[other_rows] = strict_lower(gathered_sib[k, :, 0:8].reshape(128, LEN), other * 128)

    def spectrum_start():
        def send(d, c):
            remote(SG, sg_all.at[chip], sg_send, sg_sem, chip_dev(peer(d))).start()
            return c

        lax.fori_loop(1, CHIPS, send, 0)
        pltpu.make_async_copy(SG, sg_all.at[chip], sg_sem).start()

    def spectrum_swap():
        wait_bytes(sg_all, sg_sem)
        remote(sg_all, sg_sib, sgx_send, sgx_sem, sibling).start()

    def spectrum_write():
        wait_bytes(sg_sib, sgx_sem)

        def rows(q, c):
            at = pl.ds(pl.multiple_of(q * 16, 16), 16)
            for ch in range(CHUNKS):
                out_spec[at, lanes_of(core, ch)] = sg_all[q, ch]
                out_spec[at, lanes_of(other, ch)] = sg_sib[q, ch]
            return c

        lax.fori_loop(0, CHIPS, rows, 0)

    def after(ch):
        gt, kt, vt = taps_of(gate_taps, ch), taps_of(key_taps, ch), taps_of(value_taps, ch)
        scale = spectrum[:, lanes_of(core, ch)]
        wait_bytes(F.at[ch], f_sem.at[ch])

        def regroup(j, c):
            rows = F[ch, j].reshape(LEN, 2 * LANES)
            AB[:, pl.ds(pl.multiple_of(j * 16, 16), 16)] = dot(MAT[4], rows).astype(BF16).reshape(
                16, 16, 2 * LANES
            )
            return c

        lax.fori_loop(0, CHIPS, regroup, 0)
        CARRY[...] = jnp.zeros_like(CARRY)

        def pair(step, c):
            p = CHIPS // 2 - 1 - step
            scaled = jnp.concatenate(
                [(AB[2 * p + b, :, LANES:].astype(F32) * scale).astype(BF16) for b in range(2)], 1
            )
            product = jnp.concatenate([PR[ch, block_rows(2 * p + b)] for b in range(2)], 1)
            inner_acc[...] += dot_lanes(scaled, product)
            grad_product = dot(MAT[1], scaled)
            for b in (1, 0):
                i = 2 * p + b
                x = shifted_rows(ch, i)
                gp = grad_product[:, b * LANES:(b + 1) * LANES]
                grads = (
                    CT[ch, block_rows(i)].astype(F32) * AB[i, :, :LANES].astype(F32),
                    gp * conv(vt, x),
                    gp * conv(kt, x),
                )
                for k in range(3):
                    for s in range(3):
                        TA[ch, 3 * k + s] += jnp.sum(
                            (grads[k] * x[s]).reshape(LEN // 8, 8, LANES), axis=0
                        )
                u = [gt[s] * grads[0] + kt[s] * grads[1] + vt[s] * grads[2] for s in range(3)]
                ext1 = jnp.concatenate([u[1], CARRY[0:8]], 0)
                ext2 = jnp.concatenate([u[2], CARRY[8:16]], 0)
                total = u[0] + pltpu.roll(ext1, LEN + 7, 0)[:LEN] + pltpu.roll(ext2, LEN + 6, 0)[:LEN]
                GT[ch, block_rows(i)] = total.astype(BF16)
                CARRY[0:8] = u[1][0:8]
                CARRY[8:16] = u[2][0:8]
                if b == 1:
                    @pl.when(p == CHIPS // 2 - 1)
                    def _():
                        LB[ch] = total[LEN - HALO:]
            return c

        lax.fori_loop(0, CHIPS // 2, pair, 0)
        HB[ch] = CARRY[...]

        @pl.when(chip > 0)
        def _():
            remote(HB.at[ch], HR.at[ch], hb_send.at[ch], hb_sem.at[ch], chip_dev(chip - 1)).start()

    def finish(ch):
        @pl.when(chip < CHIPS - 1)
        def _():
            wait_bytes(HR.at[ch], hb_sem.at[ch])
            row = lax.broadcasted_iota(jnp.int32, (HALO, LANES), 0)
            one, two = HR[ch, 0:8], HR[ch, 8:16]
            last = jnp.where(row == HALO - 1, one[0:1] + two[1:2], jnp.where(row == HALO - 2, two[0:1], 0.0))
            GT[ch, ROWS - HALO:ROWS] = (LB[ch] + last).astype(BF16)

        pltpu.make_async_copy(GT.at[ch, my_rows], out_tok.at[:, lanes_of(core, ch)], out_local.at[ch]).start()
        theirs = pl.ds(pl.multiple_of(other * OWN, OWN), OWN)
        remote(
            GT.at[ch, theirs], out_tok.at[:, lanes_of(core, ch)], out_send.at[ch], out_recv.at[ch], sibling
        ).start()

    sibling_sum_start(0, outer_acc)
    spectrum_start()
    after(0)
    scatter_start(0, outer_acc, lambda: None)
    spectrum_swap()
    after(1)
    finish(0)
    gather_start(0)
    spectrum_write()
    after(2)

    def put_taps():
        for n in range(9 * CHUNKS):
            k, ch = n // CHUNKS, n % CHUNKS
            piece = jnp.sum(TA[ch, k], axis=0, keepdims=True)
            red_send[1, n // 2, 8 + n % 2:9 + n % 2, 0:LANES] = piece

    sibling_sum_start(1, inner_acc)
    finish(1)
    swap_start(0)
    scatter_start(1, inner_acc, put_taps)
    finish(2)
    write_matrix(0, out_outer)
    gather_start(1)
    swap_start(1)
    write_matrix(1, out_inner)
    for n in range(9 * CHUNKS):
        k, ch = n // CHUNKS, n % CHUNKS
        out = (out_gate, out_key, out_value)[k // 3]
        row, at = slice(k % 3, k % 3 + 1), slice(8 + n % 2, 9 + n % 2)
        out[row, lanes_of(core, ch)] = gathered[1, n // 2, at, 0:LANES]
        out[row, lanes_of(other, ch)] = gathered_sib[1, n // 2, at, 0:LANES]

    for ch in range(CHUNKS):
        wait_bytes(T.at[ch, pl.ds(0, OWN)], in_send.at[ch, 0])
        wait_bytes(CT.at[ch, pl.ds(0, OWN)], in_send.at[ch, 1])

        @pl.when(chip < CHIPS - 1)
        def _():
            wait_bytes(T.at[ch, pl.ds(0, HALO)], halo_send.at[ch])

        @pl.when(chip > 0)
        def _():
            wait_bytes(HB.at[ch], hb_send.at[ch])

        wait_bytes(S.at[ch, pl.ds(0, CHIPS - 1)], s_send.at[ch])
        wait_bytes(F.at[ch, pl.ds(0, CHIPS - 1)], r_send.at[ch])
        wait_bytes(GT.at[ch, pl.ds(0, OWN)], out_local.at[ch])
        wait_bytes(GT.at[ch, pl.ds(0, OWN)], out_send.at[ch])
        wait_bytes(GT.at[ch, pl.ds(0, OWN)], out_recv.at[ch])
    for k in range(2):
        wait_bytes(sib_sum.at[k], sib_send.at[k])
        wait_bytes(red_send.at[k, pl.ds(0, CHIPS - 1)], rs_send.at[k])
        wait_bytes(gathered.at[k, pl.ds(0, CHIPS - 1)], ag_send.at[k])
        wait_bytes(gathered.at[k], gx_send.at[k])
    wait_bytes(sg_all.at[pl.ds(0, CHIPS - 1)], sg_send)
    wait_bytes(sg_all, sgx_send)


def body(tokens, cotangent, gate_taps, key_taps, value_taps, inner_mix, outer_mix, spectrum):
    shape = tokens.shape
    channels = shape[2]
    anywhere = pl.BlockSpec(memory_space=pl.ANY)
    vmem = pl.BlockSpec(memory_space=pltpu.VMEM)
    dma = pltpu.SemaphoreType.DMA
    taps_shape = jax.ShapeDtypeStruct((3, channels), F32)
    matrix = jax.ShapeDtypeStruct((LEN, LEN), F32)
    scratch = [
        pltpu.VMEM((CHUNKS, HALO + ROWS, LANES), BF16),
        pltpu.VMEM((CHUNKS, ROWS, LANES), BF16),
        pltpu.VMEM((CHUNKS, ROWS, LANES), BF16),
        pltpu.VMEM((CHIPS, LEN, 2 * LANES), BF16),
        pltpu.VMEM((CHUNKS, CHIPS, 16, 16, 2 * LANES), BF16),
        pltpu.VMEM((CHUNKS, 16, LEN, 2 * LANES), BF16),
        pltpu.VMEM((CHUNKS, 16, LEN, 2 * LANES), BF16),
        pltpu.VMEM((CHUNKS, CHIPS, 16, 16, 2 * LANES), BF16),
        pltpu.VMEM((CHUNKS, ROWS, LANES), BF16),
        pltpu.VMEM((5, LEN, LEN), BF16),
        pltpu.VMEM((16, LANES), F32),
        pltpu.VMEM((CHUNKS, 16, LANES), F32),
        pltpu.VMEM((CHUNKS, 16, LANES), F32),
        pltpu.VMEM((CHUNKS, HALO, LANES), F32),
        pltpu.VMEM((CHUNKS, 9, 8, LANES), F32),
        pltpu.VMEM((LEN, LEN), F32),
        pltpu.VMEM((LEN, LEN), F32),
        pltpu.VMEM((CHUNKS, 16, LANES), F32),
        pltpu.VMEM((2, 128, LEN), F32),
        pltpu.VMEM((2, CHIPS, 16, LEN), F32),
        pltpu.VMEM((2, CHIPS, 16, LEN), F32),
        pltpu.VMEM((2, 16, LEN), F32),
        pltpu.VMEM((2, CHIPS, 16, LEN), F32),
        pltpu.VMEM((2, CHIPS, 16, LEN), F32),
        pltpu.VMEM((CHIPS, CHUNKS, 16, LANES), F32),
        pltpu.VMEM((CHIPS, CHUNKS, 16, LANES), F32),
        dma((CHUNKS, 2)), dma((CHUNKS, 2)),
        dma((CHUNKS,)), dma((CHUNKS,)),
        dma((CHUNKS,)), dma((CHUNKS,)),
        dma((CHUNKS,)), dma((CHUNKS,)),
        dma((CHUNKS,)), dma((CHUNKS,)),
        dma((CHUNKS,)), dma((CHUNKS,)), dma((CHUNKS,)),
        dma((2,)), dma((2,)),
        dma((2,)), dma((2,)),
        dma((2,)), dma((2,)),
        dma((2,)), dma((2,)),
        dma, dma,
        dma, dma,
    ]
    outs = pl.pallas_call(
        kernel,
        out_shape=(
            jax.ShapeDtypeStruct((OWN, channels), BF16),
            taps_shape, taps_shape, taps_shape, matrix, matrix,
            jax.ShapeDtypeStruct((LEN, channels), F32),
        ),
        in_specs=[anywhere] * 2 + [vmem] * 6,
        out_specs=(anywhere,) + (vmem,) * 6,
        scratch_shapes=scratch,
        compiler_params=pltpu.CompilerParams(
            collective_id=0, has_side_effects=True, vmem_limit_bytes=60 * 1024 * 1024
        ),
        cost_estimate=pl.CostEstimate(flops=8 * 10**9, bytes_accessed=12 * 10**6, transcendentals=0),
        name="monarch",
    )(
        tokens.reshape(OWN, channels), cotangent.reshape(OWN, channels),
        gate_taps, key_taps, value_taps, inner_mix, outer_mix, spectrum,
    )
    return (outs[0].reshape(shape),) + tuple(outs[1:])


def solution(mesh):
    in_specs = (
        P(("batch", "seq"), None, None),
        P(("batch", "seq"), None, None),
        P(),
        P(),
        P(),
        P(),
        P(),
        P(),
    )
    out_specs = (
        P(("batch", "seq"), None, None),
        P("batch", None),
        P("batch", None),
        P("batch", None),
        P("batch", None),
        P("batch", None),
        P("batch", None),
    )
    return jax.shard_map(body, mesh=mesh, in_specs=in_specs, out_specs=out_specs, check_vma=False)
```

time: 846 us -> 365 us (0.43)
  waiting for transfers between devices: 457 us -> 0 us
  Pallas kernels: 0 us -> 353 us
  blocking collectives: 208 us -> 0 us
  other arithmetic: 54.3 us -> 0 us
  starting transfers between devices: 49.9 us -> 0 us
  matrix products: 28.4 us -> 0 us
  local copies, waits for them, and re-layouts: 33.6 us -> 7.97 us
  between operations: 14.4 us -> 0.7 us
    pallas_call x0 -> x1, Pallas kernels: none -> 353 us  [body(): pl.pallas_call(kernel, out_shape=(jax.ShapeDtypeStruct((OWN, channels), B...]
    psum x1 -> x0, waiting for transfers between devices: 315 us -> none  [body(): lax.psum((taps_grad(grad_gate, padded), taps_grad(grad_key, padded), taps...]
    psum x1 -> x0, blocking collectives: 144 us -> none  [body(): lax.psum((taps_grad(grad_gate, padded), taps_grad(grad_key, padded), taps...]
    all_to_all x3 -> x0, waiting for transfers between devices: 142 us -> none  [the longest x1 72.1 us: body(): lax.all_to_all(grad_inner_cols, 'seq', split_axis=0, concat_axis=1, tiled...]
    all_to_all x1 -> x0, blocking collectives: 63.3 us -> none  [body(): lax.all_to_all(inner_out, 'seq', split_axis=1, concat_axis=0, tiled=True)]
    all_to_all x3 -> x0, starting transfers between devices: 43.9 us -> none  [the longest x1 20.2 us: body(): lax.all_to_all(mixed_cols, 'seq', split_axis=0, concat_axis=1, tiled=True)]
    convert_element_type x5 -> x0, other arithmetic: 38.5 us -> none  [the longest x1 22.1 us: body(): grad_rows.reshape(block_count, block_len, channels).astype(jnp.bfloat16)]
    dot_general x6 -> x0, matrix products: 28.4 us -> none  [the longest x1 7.88 us: body(): jnp.einsum('jk,ikc->ijc', first_mix, product, preferred_element_type=jnp....]
  transfers between devices with their start and end apart: 8 -> 0, of which waited for: 3 -> 0; matrix products, arithmetic and copies ran while one was open for 3% -> 0% of each run, Pallas kernels for 0% -> 0%
where the time goes in v1:
time: 365 us; the launch traced here: 362 us
  Pallas kernels  353 us (97%)
  local copies, waits for them, and re-layouts  7.97 us (2%)
    pallas_call x1, Pallas kernels, body(): pl.pallas_call(kernel, out_shape=(jax.ShapeDtypeStruct((OWN, channels), B...  353 us
    unnamed x19, local copies, waits for them, and re-layouts  7.97 us

profile of v1, /device:TPU:8, one launch (start us, length us, event | category | flops | bytes accessed | tf_op | source)
XLA Modules:
  0.0 361.6 jit_solution(9792052821249929681)
XLA Ops:
  0.6 352.9 %monarch.1 = (bf16[2048,768]{1,0:T(8,128)(2,1)}, f32[3,768]{1,0:T(4,128)}, f32[3,768]{1,0:T(4,128)}, f32[3,768]{1,0:T(4,128)}, f32[256,256]{1,0:T(8,128)}, /*index=5*/f32[256,256]{1,0:T(8,128)}, f32[256,768]{1,0:T(8,128)}) custom-call(bf16[2048,768]{1,0:T(8,128)(2,1)} %bitcast.4, bf16[2048,768]{1,0:T(8,128)(2,1)} %bitcast.5, f32[3,768]{1,0:T(4,128)} %gate_taps.1, ...), custom_call_target="tpu_custom_call" | custom-call | flops 8000000000 | bytes 12000000 | tf_op jit(solution)/shard_map/monarch/pallas_call | solution.py:469
  353.6 0.0 copy-start.5
  353.6 0.0 copy-start.4
  353.6 0.0 copy-start.3
  353.6 0.0 copy-start.2
  353.6 0.0 copy-start.1
  353.6 0.0 copy-start
  353.6 3.9 %copy.22 = bf16[8,256,768]{2,1,0:T(8,128)(2,1)} copy(bf16[8,256,768]{2,1,0:T(8,128)(2,1)} %bitcast.3) | data formatting | bytes 6291456
  357.5 0.0 copy-done.5
  357.5 0.6 copy.23
  358.1 0.0 copy-done.4
  358.1 0.6 copy.24
  358.7 0.0 copy-done.3
  358.7 0.6 copy.25
  359.3 0.0 copy-done.2
  359.3 0.7 copy.26
  360.0 0.0 copy-done.1
  360.0 0.7 copy.27
  360.7 0.0 copy-done
  360.7 0.9 copy.28
Async XLA Ops:
  353.6 3.9 %copy-start.5 = (f32[3,768]{1,0:T(4,128)S(1)}, f32[3,768]{1,0:T(4,128)}, u32[]{:S(2)}) copy-start(f32[3,768]{1,0:T(4,128)} %get-tuple-element.29) | copy-start | bytes 27652
  353.6 4.5 %copy-start.4 = (f32[3,768]{1,0:T(4,128)S(1)}, f32[3,768]{1,0:T(4,128)}, u32[]{:S(2)}) copy-start(f32[3,768]{1,0:T(4,128)} %get-tuple-element.30) | copy-start | bytes 27652
  353.6 5.1 %copy-start.3 = (f32[3,768]{1,0:T(4,128)S(1)}, f32[3,768]{1,0:T(4,128)}, u32[]{:S(2)}) copy-start(f32[3,768]{1,0:T(4,128)} %get-tuple-element.31) | copy-start | bytes 27652
  353.6 5.7 %copy-start.2 = (f32[256,256]{1,0:T(8,128)S(1)}, f32[256,256]{1,0:T(8,128)}, u32[]{:S(2)}) copy-start(f32[256,256]{1,0:T(8,128)} %get-tuple-element.32) | copy-start | bytes 786436
  353.6 6.4 %copy-start.1 = (f32[256,256]{1,0:T(8,128)S(1)}, f32[256,256]{1,0:T(8,128)}, u32[]{:S(2)}) copy-start(f32[256,256]{1,0:T(8,128)} %get-tuple-element.33) | copy-start | bytes 786436
  353.6 7.1 %copy-start = (f32[256,768]{1,0:T(8,128)S(1)}, f32[256,768]{1,0:T(8,128)}, u32[]{:S(2)}) copy-start(f32[256,768]{1,0:T(8,128)} %get-tuple-element.34) | copy-start | bytes 2359300

commit v2 on v1

--- a/solution.py
+++ b/solution.py
@@ -17,6 +17,64 @@
 ROWS = CHIPS * LEN
 OWN = ROWS // 2
 HALO = 16
+SUB = 8
+SPLIT = 16 // SUB
+PER_CHUNK = 4 * SPLIT
+UNITS = PER_CHUNK * CHUNKS
+AHEAD = 1
+TURNS = UNITS // 3
+LAGS = (0, 1, 2, 3)
+PART = 64
+OWN_AT, ONE, TWO, PASS = 0, 1, 2, 3
+
+Y, G = 0, 1
+ROUTES = (
+    (
+        (Y, 1, 0, 1, OWN_AT, ONE, 2), (Y, 1, 1, 2, OWN_AT, ONE, 3), (Y, 2, 1, 2, ONE, TWO, 3), (Y, 3, 2, 3, PASS, ONE, 4),
+        (G, 1, 3, 2, OWN_AT, ONE, 2), (G, 1, 2, 1, OWN_AT, ONE, 3), (G, 2, 2, 1, ONE, TWO, 3), (G, 3, 1, 0, PASS, ONE, 4),
+    ),
+    (
+        (Y, 1, 0, 3, OWN_AT, TWO, 2), (Y, 1, 0, 1, OWN_AT, ONE, 4), (Y, 1, 1, 2, OWN_AT, ONE, 3), (Y, 2, 3, 2, TWO, TWO, 3),
+        (Y, 3, 2, 3, PASS, ONE, 4),
+        (G, 1, 3, 0, OWN_AT, TWO, 2), (G, 1, 3, 2, OWN_AT, ONE, 4), (G, 1, 2, 1, OWN_AT, ONE, 3), (G, 2, 0, 1, TWO, TWO, 3),
+        (G, 3, 1, 0, PASS, ONE, 4),
+    ),
+    (
+        (Y, 1, 0, 3, OWN_AT, ONE, 3), (Y, 1, 0, 1, OWN_AT, ONE, 4), (Y, 1, 1, 2, OWN_AT, ONE, 3),
+        (Y, 3, 3, 2, PASS, TWO, 4), (Y, 3, 2, 3, PASS, TWO, 4),
+        (G, 1, 3, 2, OWN_AT, ONE, 3), (G, 1, 2, 3, OWN_AT, ONE, 3), (G, 1, 1, 0, OWN_AT, ONE, 4),
+        (G, 3, 2, 1, PASS, ONE, 4), (G, 3, 3, 0, PASS, TWO, 4),
+    ),
+)
+ROUTE_KIND = (0, 0, 1)
+NONE, SUM = -1, -2
+OWN_Y = (
+    ((0, 1, 2, 3), (0, 1, 2, 3), (NONE, 0, 1, SUM), (NONE, NONE, 0, NONE)),
+    ((0, 1, 2, 3), (0, 1, 2, 3), (NONE, 0, 1, 0), (NONE, NONE, SUM, SUM)),
+)
+PASS_Y = (
+    ((0, 0, 3, 0), (NONE, NONE, 2, NONE), (NONE, NONE, 1, NONE), (NONE, NONE, 0, NONE)),
+    ((0, 0, 3, 2), (NONE, NONE, 2, NONE), (NONE, NONE, 1, 0), (NONE, NONE, NONE, NONE)),
+)
+OWN_G = (
+    ((0, 1, 2, 3), (0, 1, 2, 3), (SUM, 2, 3, NONE), (NONE, 3, NONE, NONE)),
+    ((0, 1, 2, 3), (0, 1, 2, 3), (1, SUM, 3, NONE), (SUM, NONE, NONE, NONE)),
+)
+PASS_G = (
+    ((0, 0, 0, 0), (NONE, 1, NONE, NONE), (NONE, 2, NONE, NONE), (NONE, 3, NONE, NONE)),
+    ((0, 0, 1, 0), (NONE, NONE, 2, 3), (NONE, NONE, 3, 2), (NONE, NONE, NONE, NONE)),
+)
+OUTER_ROWS = (((0, 1, 2, 3), (NONE, NONE, 3, NONE)), ((0, 1, 2, 3), (NONE, NONE, 3, 2)))
+OUTER_COLS = (
+    (
+        ((0, 1, 2, 3), (NONE, 0, 1, NONE), (NONE, NONE, 0, NONE)),
+        ((NONE, NONE, 2, NONE), (NONE, NONE, 1, NONE), (NONE, NONE, 0, NONE)),
+    ),
+    (
+        ((0, 1, 2, 3), (NONE, 0, 1, 0), (NONE, NONE, NONE, NONE)),
+        ((NONE, NONE, 2, NONE), (NONE, NONE, 1, 0), (NONE, NONE, NONE, NONE)),
+    ),
+)
 
 
 def dot(a, b):
@@ -36,12 +94,12 @@
 def kernel(
     tok, cot, gate_taps, key_taps, value_taps, inner_mix, outer_mix, spectrum,
     out_tok, out_gate, out_key, out_value, out_inner, out_outer, out_spec,
-    T, CT, PR, AB, S, Z, R, F, GT, MAT, CARRY, HB, HR, LB, TA,
-    inner_acc, outer_acc, SG, sib_sum, red_send, red_recv, red_sum, gathered, gathered_sib,
+    T, CT, AB, S, W, PS, F, GT, MAT, MIX, CARRY, HB, HR, LB, TA,
+    inner_acc, outer_acc, outer_parts, SGP, SGR, SG, red_send, red_recv, red_sum, red_sib, total, gathered,
     sg_all, sg_sib,
-    in_sem, in_send, halo_sem, halo_send, z_sem, s_send, f_sem, r_send, hb_sem, hb_send,
+    in_sem, in_send, halo_sem, halo_send, x_sem, x_send, z_sem, z_send, f_sem, r_send, hb_sem, hb_send,
     out_local, out_send, out_recv, sib_sem, sib_send, rs_sem, rs_send, ag_sem, ag_send,
-    gx_sem, gx_send, sg_sem, sg_send, sgx_sem, sgx_send,
+    sp_sem, sp_send, sg_sem, sg_send, sgx_sem, sgx_send,
 ):
     batch = lax.axis_index("batch")
     seq = lax.axis_index("seq")
@@ -58,6 +116,23 @@
     def peer(d):
         return ((cz + d // 4) % 4) * 4 + (cx + d % 4) % 4
 
+    def on_plane(x):
+        return chip_dev(cz * 4 + x)
+
+    def at_plane(values):
+        out = jnp.int32(values[3])
+        for plane in range(3):
+            out = jnp.where(cz == plane, jnp.int32(values[plane]), out)
+        return out
+
+    def clear(u, carry):
+        def rows(j, c):
+            W[u, j, PART:] = jnp.zeros((2 * PART, 2 * LANES), BF16)
+            return c
+
+        return lax.fori_loop(0, SUB, rows, carry)
+
+    lax.fori_loop(0, UNITS, clear, 0)
     barrier = pltpu.get_barrier_semaphore()
 
     def greet(d, carry):
@@ -101,8 +176,26 @@
         MAT[at] = full.astype(BF16)
         MAT[at + 1] = jnp.transpose(full).astype(BF16)
     MAT[4] = jnp.where(col_id == (row_id % 16) * 16 + row_id // 16, 1.0, 0.0).astype(BF16)
+    slot_row = lax.broadcasted_iota(jnp.int32, (LEN, 3 * PART), 0)
+    slot_col = lax.broadcasted_iota(jnp.int32, (LEN, 3 * PART), 1)
+    eye_row = lax.broadcasted_iota(jnp.int32, (PART, 3 * PART), 0)
+    eye_col = lax.broadcasted_iota(jnp.int32, (PART, 3 * PART), 1)
+    for kind in range(2):
+        for n, (table, mat) in enumerate(((OWN_Y, 2), (PASS_Y, 2), (OWN_G, 3), (PASS_G, 3))):
+            to, *slots = table[kind]
+            pick = jnp.zeros((LEN, 3 * PART), F32)
+            add = jnp.zeros((PART, 3 * PART), F32)
+            for k, planes in enumerate(slots):
+                plane = at_plane(planes)
+                here = jnp.logical_and(slot_col // PART == k, slot_row == plane * PART + slot_col % PART)
+                pick = jnp.where(here, 1.0, pick)
+                same = jnp.logical_and(eye_col == eye_row + k * PART, plane == SUM)
+                add = jnp.where(same, 1.0, add)
+            rows = MAT[mat, pl.ds(pl.multiple_of(at_plane(to) * PART, PART), PART)]
+            MIX[kind, n] = (dot(rows, pick.astype(BF16)) + add).astype(BF16)
     inner_acc[...] = jnp.zeros_like(inner_acc)
     outer_acc[...] = jnp.zeros_like(outer_acc)
+    outer_parts[...] = jnp.zeros_like(outer_parts)
     TA[...] = jnp.zeros_like(TA)
 
     def send_halo(ch, carry):
@@ -152,7 +245,6 @@
                 i = 2 * p + b
                 x = shifted_rows(ch, i)
                 product = (conv(kt, x) * conv(vt, x)).astype(BF16)
-                PR[ch, block_rows(i)] = product
                 products.append(product)
                 grad_mixed = CT[ch, block_rows(i)].astype(F32) * conv(gt, x)
                 AB[i, :, LANES:] = grad_mixed.astype(BF16)
@@ -164,75 +256,146 @@
 
         lax.fori_loop(0, CHIPS // 2, pair, 0)
 
-        def regroup(j, c):
-            rows = AB[:, pl.ds(pl.multiple_of(j * 16, 16), 16)].reshape(LEN, 2 * LANES)
-            S[ch, j] = dot(MAT[4], rows).astype(BF16).reshape(16, 16, 2 * LANES)
-            return c
-
-        lax.fori_loop(0, CHIPS, regroup, 0)
-        mine = pl.ds(pl.multiple_of(chip * 16, 16), 16)
+        def quarter(t, c):
+            u0 = ch * PER_CHUNK + t * SPLIT
+
+            def regroup(x, c):
+                j = 4 * x + t
+                rows = AB[:, pl.ds(pl.multiple_of(j * 16, 16), 16)].reshape(LEN, 2 * LANES)
+                made = dot(MAT[4], rows).astype(BF16).reshape(16, 16, 2 * LANES)
+                for h in range(SPLIT):
+                    S[u0 + h, x] = made[h * SUB:(h + 1) * SUB]
+                return c
+
+            lax.fori_loop(0, 4, regroup, 0)
+
+            return c
+
+        lax.fori_loop(0, 4, quarter, 0)
+        return carry
+
+    def slot(ref, u, k, array):
+        return ref.at[u, :, k * PART:(k + 1) * PART, array * LANES:(array + 1) * LANES]
+
+    def sends(u, route, step):
+        for array, when, source, target, here, there, _ in ROUTES[route]:
+            if when == step:
+                @pl.when(cz == source)
+                def _(array=array, target=target, here=here, there=there):
+                    origin = slot(PS, u, 0, array) if here == PASS else slot(W, u, here, array)
+                    remote(
+                        origin, slot(W, u, there, array), z_send.at[u],
+                        z_sem.at[u, 2 * array + there - 1], chip_dev(target * 4 + cx),
+                    ).start()
+
+    def receives(u, route, step):
+        for array, _, _, target, _, there, when in ROUTES[route]:
+            if when == step:
+                @pl.when(cz == target)
+                def _(array=array, there=there):
+                    wait_bytes(slot(W, u, there, array), z_sem.at[u, 2 * array + there - 1])
+
+    def pair_of(u, j, array, rows=3 * PART):
+        lanes = slice(array * LANES, (array + 1) * LANES)
+        return jnp.concatenate([W[u, j, 0:rows, lanes], W[u, j + 1, 0:rows, lanes]], 1)
+
+    def hand_out(u):
+        mine = pl.ds(pl.multiple_of(cx * 16, 16), 16)
 
         def send(d, c):
-            q = peer(d)
-            remote(S.at[ch, q], Z.at[ch, :, mine], s_send.at[ch], z_sem.at[ch], chip_dev(q)).start()
-            return c
-
-        lax.fori_loop(1, CHIPS, send, 0)
-        pltpu.make_async_copy(S.at[ch, chip], Z.at[ch, :, mine], z_sem.at[ch]).start()
-        return carry
-
-    lax.fori_loop(0, CHUNKS, before, 0)
-
-    def across(ch, carry):
-        wait_bytes(Z.at[ch], z_sem.at[ch])
-        scale = spectrum[pl.ds(pl.multiple_of(chip * 16, 16), 16), lanes_of(core, ch)]
+            x = (cx + d) % 4
+            remote(S.at[u, x], W.at[u, :, mine], x_send.at[u], x_sem.at[u], on_plane(x)).start()
+            return c
+
+        lax.fori_loop(1, 4, send, 0)
+        pltpu.make_async_copy(S.at[u, cx], W.at[u, :, mine], x_sem.at[u]).start()
+
+    def step1(u, route):
+        wait_bytes(W.at[u, :, 0:PART], x_sem.at[u])
+        sends(u, route, 1)
+
+    def step2(u, route):
+        receives(u, route, 2)
+        sends(u, route, 2)
+
+    def step3(u, route):
+        receives(u, route, 3)
+        kind = ROUTE_KIND[route]
+        for array in (Y, G):
+            single = 2 if array == Y else 1
+            used = (3 if kind == 0 else 2) * PART
+            passes = cz == single if kind == 0 else cz >= 2
+
+            @pl.when(passes)
+            def _(array=array):
+                def pair(p, c):
+                    j = 2 * p
+                    mix = MIX[kind, 2 * array + 1, :, 0:used]
+                    total = dot(mix, pair_of(u, j, array, used)).astype(BF16)
+                    for b in range(2):
+                        PS[u, j + b, :, array * LANES:(array + 1) * LANES] = total[:, b * LANES:(b + 1) * LANES]
+                    return c
+
+                lax.fori_loop(0, SUB // 2, pair, 0)
+        sends(u, route, 3)
+
+    def step4(u, route):
+        receives(u, route, 4)
+        kind = ROUTE_KIND[route]
+        ch, t, h = u // PER_CHUNK, (u % PER_CHUNK) // SPLIT, u % SPLIT
+        back = F.at[ch, 4 * cx + t, pl.ds(h * SUB, SUB)]
 
         def pair(p, c):
             j = 2 * p
-            z0, z1 = Z[ch, j], Z[ch, j + 1]
-            inner = jnp.concatenate([z0[:, :LANES], z1[:, :LANES]], 1)
-            grads = jnp.concatenate([z0[:, LANES:], z1[:, LANES:]], 1)
-            mixed = dot(MAT[2], inner).astype(BF16)
-            grad_inner = dot(MAT[3], grads).astype(BF16)
-            outer_acc[...] += dot_lanes(grads, inner)
-            terms = jnp.sum(grad_inner.astype(F32) * inner.astype(F32), axis=0, keepdims=True)
+            inner, grads = pair_of(u, j, Y), pair_of(u, j, G)
+            mixed = dot(MIX[kind, 0], inner).astype(BF16)
+            grad_inner = dot(MIX[kind, 2], grads).astype(BF16)
+            outer_parts[kind, :, 0:3 * PART] += dot_lanes(grads[0:2 * PART], inner)
+            terms = jnp.sum(
+                grad_inner.astype(F32) * inner[0:PART].astype(F32), axis=0, keepdims=True
+            )
             for b in range(2):
                 at = slice(b * LANES, (b + 1) * LANES)
-                R[ch, j + b, :, :LANES] = mixed[:, at]
-                R[ch, j + b, :, LANES:] = grad_inner[:, at]
-                SG[ch, pl.ds(j + b, 1)] = terms[:, at]
-            return c
-
-        lax.fori_loop(0, 8, pair, 0)
-        SG[ch] = SG[ch] / scale
+                S[u, :, j + b, :, :LANES] = mixed[:, at].reshape(4, 16, LANES)
+                S[u, :, j + b, :, LANES:] = grad_inner[:, at].reshape(4, 16, LANES)
+                SGP[t, ch, pl.ds(h * SUB + j + b, 1)] = terms[:, at]
+            return c
+
+        wait_bytes(S.at[u, pl.ds(0, 3)], x_send.at[u])
+        lax.fori_loop(0, SUB // 2, pair, 0)
 
         def send(d, c):
-            q = peer(d)
+            x = (cx + d) % 4
             remote(
-                R.at[ch, :, pl.ds(pl.multiple_of(q * 16, 16), 16)], F.at[ch, chip],
-                r_send.at[ch], f_sem.at[ch], chip_dev(q),
+                S.at[u, x], back,
+                r_send.at[ch], f_sem.at[ch], on_plane(x),
             ).start()
             return c
 
-        lax.fori_loop(1, CHIPS, send, 0)
+        lax.fori_loop(1, 4, send, 0)
         pltpu.make_async_copy(
-            R.at[ch, :, pl.ds(pl.multiple_of(chip * 16, 16), 16)], F.at[ch, chip], f_sem.at[ch]
+            S.at[u, cx], back, f_sem.at[ch]
         ).start()
-        return carry
-
-    lax.fori_loop(0, CHUNKS, across, 0)
-
-    half_rows = pl.ds(pl.multiple_of(core * 128, 128), 128)
-    other_rows = pl.ds(pl.multiple_of(other * 128, 128), 128)
-
-    def sibling_sum_start(k, acc):
-        remote(acc.at[other_rows], sib_sum.at[k], sib_send.at[k], sib_sem.at[k], sibling).start()
+
+    def place_outer():
+        cols = lax.broadcasted_iota(jnp.int32, (PART, LEN), 1)
+        for kind in range(2):
+            for k in range(2):
+                row = at_plane(OUTER_ROWS[kind][k])
+                part = outer_parts[kind, k * PART:(k + 1) * PART]
+                total = jnp.zeros((PART, LEN), F32)
+                for n, planes in enumerate(OUTER_COLS[kind][k]):
+                    plane = at_plane(planes)
+                    moved = pltpu.roll(part, (plane * PART + LEN - n * PART) % LEN, 1)
+                    total = jnp.where(cols // PART == plane, moved, total)
+
+                @pl.when(row != NONE)
+                def _(row=row, total=total):
+                    outer_acc[pl.ds(pl.multiple_of(row * PART, PART), PART)] += total
 
     def scatter_start(k, acc, extra):
-        wait_bytes(sib_sum.at[k], sib_sem.at[k])
-        total = acc[half_rows] + sib_sum[k]
-        red_send[k, :, 0:8] = total.reshape(CHIPS, 8, LEN)
-        red_send[k, :, 8:16] = jnp.zeros((CHIPS, 8, LEN), F32)
+        red_send[k, :, 0:16] = acc[...].reshape(CHIPS, 16, LEN)
+        red_send[k, :, 16:24] = jnp.zeros((CHIPS, 8, LEN), F32)
         extra()
 
         def send(d, c):
@@ -243,27 +406,44 @@
         lax.fori_loop(1, CHIPS, send, 0)
         pltpu.make_async_copy(red_send.at[k, chip], red_recv.at[k, chip], rs_sem.at[k]).start()
 
-    def gather_start(k):
+    def swap_start(k):
         wait_bytes(red_recv.at[k], rs_sem.at[k])
         red_sum[k] = jnp.sum(red_recv[k], axis=0)
+        remote(red_sum.at[k], red_sib.at[k], sib_send.at[k], sib_sem.at[k], sibling).start()
+
+    def gather_start(k):
+        wait_bytes(red_sib.at[k], sib_sem.at[k])
+        total[k, 0:16] = red_sum[k, 0:16] + red_sib[k, 0:16]
+        total[k, 16:24] = jnp.zeros((8, LEN), F32)
+        total[k, pl.ds(16 + core, 1)] = red_sum[k, 16:17]
+        total[k, pl.ds(16 + other, 1)] = red_sib[k, 16:17]
 
         def send(d, c):
-            remote(red_sum.at[k], gathered.at[k, chip], ag_send.at[k], ag_sem.at[k], chip_dev(peer(d))).start()
+            remote(total.at[k], gathered.at[k, chip], ag_send.at[k], ag_sem.at[k], chip_dev(peer(d))).start()
             return c
 
         lax.fori_loop(1, CHIPS, send, 0)
-        pltpu.make_async_copy(red_sum.at[k], gathered.at[k, chip], ag_sem.at[k]).start()
-
-    def swap_start(k):
+        pltpu.make_async_copy(total.at[k], gathered.at[k, chip], ag_sem.at[k]).start()
+
+    def write_matrix(k, out):
         wait_bytes(gathered.at[k], ag_sem.at[k])
-        remote(gathered.at[k], gathered_sib.at[k], gx_send.at[k], gx_sem.at[k], sibling).start()
-
-    def write_matrix(k, out):
-        wait_bytes(gathered_sib.at[k], gx_sem.at[k])
-        out[half_rows] = strict_lower(gathered[k, :, 0:8].reshape(128, LEN), core * 128)
-        out[other_rows] = strict_lower(gathered_sib[k, :, 0:8].reshape(128, LEN), other * 128)
+        out[...] = strict_lower(gathered[k, :, 0:16].reshape(LEN, LEN), 0)
+
+    def spectrum_scatter():
+        def send(d, c):
+            t = (cz + d) % 4
+            remote(SGP.at[t], SGR.at[cz], sp_send, sp_sem, chip_dev(t * 4 + cx)).start()
+            return c
+
+        lax.fori_loop(1, 4, send, 0)
+        pltpu.make_async_copy(SGP.at[cz], SGR.at[cz], sp_sem).start()
 
     def spectrum_start():
+        wait_bytes(SGR, sp_sem)
+        here = pl.ds(pl.multiple_of((4 * cx + cz) * 16, 16), 16)
+        for ch in range(CHUNKS):
+            SG[ch] = jnp.sum(SGR[:, ch], axis=0) / spectrum[here, lanes_of(core, ch)]
+
         def send(d, c):
             remote(SG, sg_all.at[chip], sg_send, sg_sem, chip_dev(peer(d))).start()
             return c
@@ -279,7 +459,7 @@
         wait_bytes(sg_sib, sgx_sem)
 
         def rows(q, c):
-            at = pl.ds(pl.multiple_of(q * 16, 16), 16)
+            at = pl.ds(pl.multiple_of((4 * (q % 4) + q // 4) * 16, 16), 16)
             for ch in range(CHUNKS):
                 out_spec[at, lanes_of(core, ch)] = sg_all[q, ch]
                 out_spec[at, lanes_of(other, ch)] = sg_sib[q, ch]
@@ -307,17 +487,20 @@
             scaled = jnp.concatenate(
                 [(AB[2 * p + b, :, LANES:].astype(F32) * scale).astype(BF16) for b in range(2)], 1
             )
-            product = jnp.concatenate([PR[ch, block_rows(2 * p + b)] for b in range(2)], 1)
+            shifts = [shifted_rows(ch, 2 * p + b) for b in range(2)]
+            keys = [conv(kt, x) for x in shifts]
+            values = [conv(vt, x) for x in shifts]
+            product = jnp.concatenate([(keys[b] * values[b]).astype(BF16) for b in range(2)], 1)
             inner_acc[...] += dot_lanes(scaled, product)
             grad_product = dot(MAT[1], scaled)
             for b in (1, 0):
                 i = 2 * p + b
-                x = shifted_rows(ch, i)
+                x = shifts[b]
                 gp = grad_product[:, b * LANES:(b + 1) * LANES]
                 grads = (
                     CT[ch, block_rows(i)].astype(F32) * AB[i, :, :LANES].astype(F32),
-                    gp * conv(vt, x),
-                    gp * conv(kt, x),
+                    gp * values[b],
+                    gp * keys[b],
                 )
                 for k in range(3):
                     for s in range(3):
@@ -359,38 +542,77 @@
             GT.at[ch, theirs], out_tok.at[:, lanes_of(core, ch)], out_send.at[ch], out_recv.at[ch], sibling
         ).start()
 
-    sibling_sum_start(0, outer_acc)
-    spectrum_start()
+    before(0, 0)
+
+    steps = (step1, step2, step3, step4)
+
+    def step(n, k):
+        at = k - LAGS[n - 1]
+
+        @pl.when(jnp.logical_and(at >= 0, at < TURNS))
+        def _():
+            for route in range(len(ROUTES)):
+                steps[n - 1](len(ROUTES) * at + route, route)
+
+    def hand_out_turn(at):
+        for route in range(len(ROUTES)):
+            hand_out(len(ROUTES) * at + route)
+
+    def turn(k, carry):
+        @pl.when(k + AHEAD < TURNS)
+        def _():
+            hand_out_turn(k + AHEAD)
+
+        step(2, k)
+        step(3, k)
+        step(4, k)
+        step(1, k)
+        return carry
+
+    for at in range(AHEAD):
+        hand_out_turn(at)
+    first = -(-PER_CHUNK // len(ROUTES)) + LAGS[3] + 1
+    second = -(-2 * PER_CHUNK // len(ROUTES)) + LAGS[3] + 1
+    lax.fori_loop(0, 0, turn, 0)
+    before(1, 0)
+    lax.fori_loop(0, 2, turn, 0)
+    before(2, 0)
+    lax.fori_loop(2, first, turn, 0)
     after(0)
-    scatter_start(0, outer_acc, lambda: None)
-    spectrum_swap()
+    lax.fori_loop(first, second, turn, 0)
     after(1)
     finish(0)
-    gather_start(0)
-    spectrum_write()
+    lax.fori_loop(second, TURNS + LAGS[3], turn, 0)
+    place_outer()
+    scatter_start(0, outer_acc, lambda: None)
+    spectrum_scatter()
     after(2)
 
     def put_taps():
         for n in range(9 * CHUNKS):
             k, ch = n // CHUNKS, n % CHUNKS
-            piece = jnp.sum(TA[ch, k], axis=0, keepdims=True)
-            red_send[1, n // 2, 8 + n % 2:9 + n % 2, 0:LANES] = piece
-
-    sibling_sum_start(1, inner_acc)
+            at = slice((n % 2) * LANES, (n % 2 + 1) * LANES)
+            red_send[1, n // 2, 16:17, at] = jnp.sum(TA[ch, k], axis=0, keepdims=True)
+
+    scatter_start(1, inner_acc, put_taps)
+    swap_start(0)
+    spectrum_start()
     finish(1)
-    swap_start(0)
-    scatter_start(1, inner_acc, put_taps)
+    gather_start(0)
+    swap_start(1)
     finish(2)
+    spectrum_swap()
+    gather_start(1)
     write_matrix(0, out_outer)
-    gather_start(1)
-    swap_start(1)
+    spectrum_write()
     write_matrix(1, out_inner)
     for n in range(9 * CHUNKS):
         k, ch = n // CHUNKS, n % CHUNKS
         out = (out_gate, out_key, out_value)[k // 3]
-        row, at = slice(k % 3, k % 3 + 1), slice(8 + n % 2, 9 + n % 2)
-        out[row, lanes_of(core, ch)] = gathered[1, n // 2, at, 0:LANES]
-        out[row, lanes_of(other, ch)] = gathered_sib[1, n // 2, at, 0:LANES]
+        at = slice((n % 2) * LANES, (n % 2 + 1) * LANES)
+        for c in range(2):
+            lanes = slice(c * HALF + ch * LANES, c * HALF + (ch + 1) * LANES)
+            out[k % 3:k % 3 + 1, lanes] = gathered[1, n // 2, 16 + c:17 + c, at]
 
     for ch in range(CHUNKS):
         wait_bytes(T.at[ch, pl.ds(0, OWN)], in_send.at[ch, 0])
@@ -404,18 +626,52 @@
         def _():
             wait_bytes(HB.at[ch], hb_send.at[ch])
 
-        wait_bytes(S.at[ch, pl.ds(0, CHIPS - 1)], s_send.at[ch])
-        wait_bytes(F.at[ch, pl.ds(0, CHIPS - 1)], r_send.at[ch])
+        wait_bytes(F.at[ch, pl.ds(0, 12)], r_send.at[ch])
         wait_bytes(GT.at[ch, pl.ds(0, OWN)], out_local.at[ch])
         wait_bytes(GT.at[ch, pl.ds(0, OWN)], out_send.at[ch])
         wait_bytes(GT.at[ch, pl.ds(0, OWN)], out_recv.at[ch])
+    def sent(at, carry):
+        for route, lines in enumerate(ROUTES):
+            u = len(ROUTES) * at + route
+            for source in range(4):
+                count = sum(line[2] == source for line in lines)
+
+                @pl.when(cz == source)
+                def _(count=count, u=u):
+                    wait_bytes(W.at[u, :, 0:count * PART, 0:LANES], z_send.at[u])
+
+        return carry
+
+    lax.fori_loop(0, TURNS, sent, 0)
     for k in range(2):
-        wait_bytes(sib_sum.at[k], sib_send.at[k])
+        wait_bytes(red_sum.at[k], sib_send.at[k])
         wait_bytes(red_send.at[k, pl.ds(0, CHIPS - 1)], rs_send.at[k])
         wait_bytes(gathered.at[k, pl.ds(0, CHIPS - 1)], ag_send.at[k])
-        wait_bytes(gathered.at[k], gx_send.at[k])
+    wait_bytes(SGR.at[pl.ds(0, 3)], sp_send)
     wait_bytes(sg_all.at[pl.ds(0, CHIPS - 1)], sg_send)
     wait_bytes(sg_all, sgx_send)
+
+
+def hand_over(*refs):
+    count = (len(refs) - 2) // 3
+    held, in_sem, out_sem = refs[2 * count:3 * count], refs[-2], refs[-1]
+    pieces = [(0, pl.ds(n * (OWN // 4), OWN // 4)) for n in range(4)]
+    pieces += [(n, pl.ds(0, held[n].shape[0])) for n in range(1, count)]
+    into = [
+        pltpu.make_async_copy(refs[n].at[rows], held[n].at[rows], in_sem.at[k])
+        for k, (n, rows) in enumerate(pieces)
+    ]
+    out = [
+        pltpu.make_async_copy(held[n].at[rows], refs[count + n].at[rows], out_sem.at[k])
+        for k, (n, rows) in enumerate(pieces)
+    ]
+    for copy in into:
+        copy.start()
+    for k, copy in enumerate(out):
+        into[k].wait()
+        copy.start()
+    for copy in out:
+        copy.wait()
 
 
 def body(tokens, cotangent, gate_taps, key_taps, value_taps, inner_mix, outer_mix, spectrum):
@@ -429,14 +685,14 @@
     scratch = [
         pltpu.VMEM((CHUNKS, HALO + ROWS, LANES), BF16),
         pltpu.VMEM((CHUNKS, ROWS, LANES), BF16),
-        pltpu.VMEM((CHUNKS, ROWS, LANES), BF16),
         pltpu.VMEM((CHIPS, LEN, 2 * LANES), BF16),
-        pltpu.VMEM((CHUNKS, CHIPS, 16, 16, 2 * LANES), BF16),
-        pltpu.VMEM((CHUNKS, 16, LEN, 2 * LANES), BF16),
-        pltpu.VMEM((CHUNKS, 16, LEN, 2 * LANES), BF16),
+        pltpu.VMEM((UNITS, 4, SUB, 16, 2 * LANES), BF16),
+        pltpu.VMEM((UNITS, SUB, 3 * PART, 2 * LANES), BF16),
+        pltpu.VMEM((UNITS, SUB, PART, 2 * LANES), BF16),
         pltpu.VMEM((CHUNKS, CHIPS, 16, 16, 2 * LANES), BF16),
         pltpu.VMEM((CHUNKS, ROWS, LANES), BF16),
         pltpu.VMEM((5, LEN, LEN), BF16),
+        pltpu.VMEM((2, 4, PART, 3 * PART), BF16),
         pltpu.VMEM((16, LANES), F32),
         pltpu.VMEM((CHUNKS, 16, LANES), F32),
         pltpu.VMEM((CHUNKS, 16, LANES), F32),
@@ -444,25 +700,29 @@
         pltpu.VMEM((CHUNKS, 9, 8, LANES), F32),
         pltpu.VMEM((LEN, LEN), F32),
         pltpu.VMEM((LEN, LEN), F32),
+        pltpu.VMEM((2, 2 * PART, LEN), F32),
+        pltpu.VMEM((4, CHUNKS, 16, LANES), F32),
+        pltpu.VMEM((4, CHUNKS, 16, LANES), F32),
         pltpu.VMEM((CHUNKS, 16, LANES), F32),
-        pltpu.VMEM((2, 128, LEN), F32),
-        pltpu.VMEM((2, CHIPS, 16, LEN), F32),
-        pltpu.VMEM((2, CHIPS, 16, LEN), F32),
-        pltpu.VMEM((2, 16, LEN), F32),
-        pltpu.VMEM((2, CHIPS, 16, LEN), F32),
-        pltpu.VMEM((2, CHIPS, 16, LEN), F32),
+        pltpu.VMEM((2, CHIPS, 24, LEN), F32),
+        pltpu.VMEM((2, CHIPS, 24, LEN), F32),
+        pltpu.VMEM((2, 24, LEN), F32),
+        pltpu.VMEM((2, 24, LEN), F32),
+        pltpu.VMEM((2, 24, LEN), F32),
+        pltpu.VMEM((2, CHIPS, 24, LEN), F32),
         pltpu.VMEM((CHIPS, CHUNKS, 16, LANES), F32),
         pltpu.VMEM((CHIPS, CHUNKS, 16, LANES), F32),
         dma((CHUNKS, 2)), dma((CHUNKS, 2)),
         dma((CHUNKS,)), dma((CHUNKS,)),
-        dma((CHUNKS,)), dma((CHUNKS,)),
+        dma((UNITS,)), dma((UNITS,)),
+        dma((UNITS, 4)), dma((UNITS,)),
         dma((CHUNKS,)), dma((CHUNKS,)),
         dma((CHUNKS,)), dma((CHUNKS,)),
         dma((CHUNKS,)), dma((CHUNKS,)), dma((CHUNKS,)),
         dma((2,)), dma((2,)),
         dma((2,)), dma((2,)),
         dma((2,)), dma((2,)),
-        dma((2,)), dma((2,)),
+        dma, dma,
         dma, dma,
         dma, dma,
     ]
@@ -477,7 +737,7 @@
         out_specs=(anywhere,) + (vmem,) * 6,
         scratch_shapes=scratch,
         compiler_params=pltpu.CompilerParams(
-            collective_id=0, has_side_effects=True, vmem_limit_bytes=60 * 1024 * 1024
+            collective_id=0, has_side_effects=True, vmem_limit_bytes=62 * 1024 * 1024
         ),
         cost_estimate=pl.CostEstimate(flops=8 * 10**9, bytes_accessed=12 * 10**6, transcendentals=0),
         name="monarch",
@@ -485,6 +745,14 @@
         tokens.reshape(OWN, channels), cotangent.reshape(OWN, channels),
         gate_taps, key_taps, value_taps, inner_mix, outer_mix, spectrum,
     )
+    outs = pl.pallas_call(
+        hand_over,
+        out_shape=tuple(jax.ShapeDtypeStruct(out.shape, out.dtype) for out in outs),
+        in_specs=[anywhere] * len(outs),
+        out_specs=(anywhere,) * len(outs),
+        scratch_shapes=[pltpu.VMEM(out.shape, out.dtype) for out in outs] + [dma((10,)), dma((10,))],
+        name="results",
+    )(*outs)
     return (outs[0].reshape(shape),) + tuple(outs[1:])
 
 

time: 365 us -> 334 us (0.915)
  Pallas kernels: 353 us -> 333 us
  local copies, waits for them, and re-layouts: 7.97 us -> 0 us
    pallas_call x1, Pallas kernels: 353 us -> 329 us  [body(): pl.pallas_call(kernel, out_shape=(jax.ShapeDtypeStruct((OWN, channels), B...]
    unnamed x19 -> x0, local copies, waits for them, and re-layouts: 7.97 us -> none
    pallas_call x0 -> x1, Pallas kernels: none -> 3.94 us  [body(): pl.pallas_call(hand_over, out_shape=tuple((jax.ShapeDtypeStruct(out.shape...]
where the time goes in v2:
time: 334 us
  Pallas kernels  333 us (100%)
    pallas_call x1, Pallas kernels, body(): pl.pallas_call(kernel, out_shape=(jax.ShapeDtypeStruct((OWN, channels), B...  329 us

profile of v2, /device:TPU:8, one launch (start us, length us, event | category | flops | bytes accessed | tf_op | source)
XLA Modules:
  0.0 333.9 jit_solution(14762396380942846509)
XLA Ops:
  0.6 329.3 %monarch.1 = (bf16[2048,768]{1,0:T(8,128)(2,1)}, f32[3,768]{1,0:T(4,128)}, f32[3,768]{1,0:T(4,128)}, f32[3,768]{1,0:T(4,128)}, f32[256,256]{1,0:T(8,128)}, /*index=5*/f32[256,256]{1,0:T(8,128)}, f32[256,768]{1,0:T(8,128)}) custom-call(bf16[2048,768]{1,0:T(8,128)(2,1)} %bitcast.3, bf16[2048,768]{1,0:T(8,128)(2,1)} %bitcast.4, f32[3,768]{1,0:T(4,128)} %gate_taps.1, ...), custom_call_target="tpu_custom_call" | custom-call | flops 8000000000 | bytes 12000000 | tf_op jit(solution)/shard_map/monarch/pallas_call | solution.py:729
  330.0 3.9 %results.1 = (bf16[2048,768]{1,0:T(8,128)(2,1)}, f32[3,768]{1,0:T(4,128)}, f32[3,768]{1,0:T(4,128)}, f32[3,768]{1,0:T(4,128)}, f32[256,256]{1,0:T(8,128)}, /*index=5*/f32[256,256]{1,0:T(8,128)}, f32[256,768]{1,0:T(8,128)}) custom-call(bf16[2048,768]{1,0:T(8,128)(2,1)} %get-tuple-element.21.refs_0_, f32[3,768]{1,0:T(4,128)} %get-tuple-element.22.refs_1_, ...), custom_call_target="tpu_custom_call" | custom-call | tf_op jit(solution)/shard_map/results/pallas_call | solution.py:748

commit v3 on v2

--- a/solution.py
+++ b/solution.py
@@ -571,8 +571,8 @@
 
     for at in range(AHEAD):
         hand_out_turn(at)
-    first = -(-PER_CHUNK // len(ROUTES)) + LAGS[3] + 1
-    second = -(-2 * PER_CHUNK // len(ROUTES)) + LAGS[3] + 1
+    first = -(-PER_CHUNK // len(ROUTES)) + LAGS[3] + 0
+    second = -(-2 * PER_CHUNK // len(ROUTES)) + LAGS[3] + 0
     lax.fori_loop(0, 0, turn, 0)
     before(1, 0)
     lax.fori_loop(0, 2, turn, 0)

time: 334 us -> 342 us (1.024)
  Pallas kernels: 333 us -> 341 us
    pallas_call x1, Pallas kernels: 329 us -> 337 us  [body(): pl.pallas_call(kernel, out_shape=(jax.ShapeDtypeStruct((OWN, channels), B...]
where the time goes in v3:
time: 342 us; the launch traced here: 341 us
  Pallas kernels  341 us (100%)
    pallas_call x1, Pallas kernels, body(): pl.pallas_call(kernel, out_shape=(jax.ShapeDtypeStruct((OWN, channels), B...  337 us

profile of v3, /device:TPU:8, one launch (start us, length us, event | category | flops | bytes accessed | tf_op | source)
XLA Modules:
  0.0 341.2 jit_solution(13020047942950471788)
XLA Ops:
  0.6 336.6 %monarch.1 = (bf16[2048,768]{1,0:T(8,128)(2,1)}, f32[3,768]{1,0:T(4,128)}, f32[3,768]{1,0:T(4,128)}, f32[3,768]{1,0:T(4,128)}, f32[256,256]{1,0:T(8,128)}, /*index=5*/f32[256,256]{1,0:T(8,128)}, f32[256,768]{1,0:T(8,128)}) custom-call(bf16[2048,768]{1,0:T(8,128)(2,1)} %bitcast.3, bf16[2048,768]{1,0:T(8,128)(2,1)} %bitcast.4, f32[3,768]{1,0:T(4,128)} %gate_taps.1, ...), custom_call_target="tpu_custom_call" | custom-call | flops 8000000000 | bytes 12000000 | tf_op jit(solution)/shard_map/monarch/pallas_call | solution.py:729
  337.2 3.9 %results.1 = (bf16[2048,768]{1,0:T(8,128)(2,1)}, f32[3,768]{1,0:T(4,128)}, f32[3,768]{1,0:T(4,128)}, f32[3,768]{1,0:T(4,128)}, f32[256,256]{1,0:T(8,128)}, /*index=5*/f32[256,256]{1,0:T(8,128)}, f32[256,768]{1,0:T(8,128)}) custom-call(bf16[2048,768]{1,0:T(8,128)(2,1)} %get-tuple-element.21.refs_0_, f32[3,768]{1,0:T(4,128)} %get-tuple-element.22.refs_1_, ...), custom_call_target="tpu_custom_call" | custom-call | tf_op jit(solution)/shard_map/results/pallas_call | solution.py:748

commit v4 on v2

--- a/solution.py
+++ b/solution.py
@@ -571,7 +571,7 @@
 
     for at in range(AHEAD):
         hand_out_turn(at)
-    first = -(-PER_CHUNK // len(ROUTES)) + LAGS[3] + 1
+    first = -(-PER_CHUNK // len(ROUTES)) + LAGS[3] + 2
     second = -(-2 * PER_CHUNK // len(ROUTES)) + LAGS[3] + 1
     lax.fori_loop(0, 0, turn, 0)
     before(1, 0)

time: 334 us -> 338 us (1.012)
  Pallas kernels: 333 us -> 337 us
    pallas_call x1, Pallas kernels: 329 us -> 333 us  [body(): pl.pallas_call(kernel, out_shape=(jax.ShapeDtypeStruct((OWN, channels), B...]
where the time goes in v4:
time: 338 us; the launch traced here: 337 us
  Pallas kernels  337 us (100%)
    pallas_call x1, Pallas kernels, body(): pl.pallas_call(kernel, out_shape=(jax.ShapeDtypeStruct((OWN, channels), B...  333 us

profile of v4, /device:TPU:8, one launch (start us, length us, event | category | flops | bytes accessed | tf_op | source)
XLA Modules:
  0.0 337.4 jit_solution(10970375584106804760)
XLA Ops:
  0.6 332.8 %monarch.1 = (bf16[2048,768]{1,0:T(8,128)(2,1)}, f32[3,768]{1,0:T(4,128)}, f32[3,768]{1,0:T(4,128)}, f32[3,768]{1,0:T(4,128)}, f32[256,256]{1,0:T(8,128)}, /*index=5*/f32[256,256]{1,0:T(8,128)}, f32[256,768]{1,0:T(8,128)}) custom-call(bf16[2048,768]{1,0:T(8,128)(2,1)} %bitcast.3, bf16[2048,768]{1,0:T(8,128)(2,1)} %bitcast.4, f32[3,768]{1,0:T(4,128)} %gate_taps.1, ...), custom_call_target="tpu_custom_call" | custom-call | flops 8000000000 | bytes 12000000 | tf_op jit(solution)/shard_map/monarch/pallas_call | solution.py:729
  333.4 3.9 %results.1 = (bf16[2048,768]{1,0:T(8,128)(2,1)}, f32[3,768]{1,0:T(4,128)}, f32[3,768]{1,0:T(4,128)}, f32[3,768]{1,0:T(4,128)}, f32[256,256]{1,0:T(8,128)}, /*index=5*/f32[256,256]{1,0:T(8,128)}, f32[256,768]{1,0:T(8,128)}) custom-call(bf16[2048,768]{1,0:T(8,128)(2,1)} %get-tuple-element.21.refs_0_, f32[3,768]{1,0:T(4,128)} %get-tuple-element.22.refs_1_, ...), custom_call_target="tpu_custom_call" | custom-call | tf_op jit(solution)/shard_map/results/pallas_call | solution.py:748
